TPU v7x, 32 devices: a whole 2x2x4 slice. The times are simulated.
32 devices in a mesh: tm: 4 (over x, core), space: 8 (over z, y).
Axes of the slice: x: 2, y: 2, z: 4, core: 2. Of those that a mesh axis runs over, the one named last changes fastest.
Arguments:
- pixels: bfloat16 [163840, 128], P(('tm', 'space')), may hold values from -48 to 48
- weights: bfloat16 [163840], P(('tm', 'space')), may hold values from 0.5 to 2
- tile_index: int32 [163840], P(('tm', 'space')), may hold values from 0 to 7, as said below
- tile_row: int32 [163840], P(('tm', 'space')), may hold values from 0 to 159, as said below
- granule_day: int32 [163840], P(('tm', 'space')), may hold values from 0 to 127
Outputs:
- field: bfloat16 [8, 160, 512, 128], P('space', 'tm')
- basis: bfloat16 [8, 160, 256, 128], P('space', 'tm')
- propagator: float32 [256, 256], replicated
Inputs may be any that keep to these rules, and one draw needn't show every extreme that they name: `tile_index`: of the rows of one device, at most 1280 name one tile, and in every device's rows some tile is named by exactly 1280. `tile_row`: of the rows of one device, at most 320 name one tile and a grid row from k * 40 to (k + 1) * 40 - 1 for one k, and in every device's rows some tile and k reach 320.
All inputs are finite; a program needn't handle non-finite values.
Results may differ from a plain program's by a relative error of at most 0.0061.
Values may be sent and summed in bfloat16 or wider, within the bound.
No kernel may reach another device: no remote copies, remote signals or barrier semaphores. Data moves between devices by JAX's collectives and lax.ppermute only.
A program may use at most 64 MiB of HBM per device.

v0:
```python
import functools
import math

import jax
import jax.numpy as jnp
from jax import lax
from jax.experimental import pallas as pl
from jax.experimental.pallas import tpu as pltpu
from jax.sharding import PartitionSpec as P

GR_DEV = 160
DAYS = 512
RANK = 256
ITERS = 8
LANES = 128
META_ROWS = 16
GROUP = 16
CLASH = 1 << 20
STEPS = 5
VMEM = 56 * 1024 * 1024

LAST_LAST = (((1,), (1,)), ((), ()))
FIRST_FIRST = (((0,), (0,)), ((), ()))


def round_up(value, unit):
    return -(-value // unit) * unit


def split_rows(slots):
    rows = round_up(slots, 16)
    return rows, rows * 13 // 20 // 16 * 16


def pack_kernel(
    dims, tile_ref, row_ref, day_ref, weight_ref, pix_ref, first_ref, last_ref, pos_v, pos_s, rows_v, meta_v, pixf, outf, mrow,
    first_v, last_v, pix_v, hot_v, prefix_v, sems
):
    time_count, space_count, rows_tm, slot_rows, first_rows, width = dims
    dest_count = time_count * space_count
    chunks = tile_ref.shape[0]
    pieces = width // LANES

    fetch = pltpu.make_async_copy(pix_ref, pix_v, sems.at[3])
    fetch.start()
    tile = tile_ref[...]
    row = row_ref[...]
    group = jnp.zeros_like(row)
    for k in range(1, time_count):
        group = group + jnp.where(row >= k * rows_tm, 1, 0)
    dest_all = group * space_count + tile
    rows_v[0] = dest_all.astype(jnp.float32)
    rows_v[2] = weight_ref[...].astype(jnp.float32)
    rows_v[3] = (row - group * rows_tm).astype(jnp.float32)
    rows_v[4] = day_ref[...].astype(jnp.float32)

    dest_iota = lax.broadcasted_iota(jnp.int32, (dest_count, LANES), 0)
    upper = jnp.where(
        lax.broadcasted_iota(jnp.int32, (LANES, LANES), 0) <= lax.broadcasted_iota(jnp.int32, (LANES, LANES), 1), 1.0, 0.0
    ).astype(jnp.bfloat16)
    for c in range(chunks):
        hot = dest_iota == dest_all[c : c + 1, :]
        hot_v[c * dest_count : (c + 1) * dest_count, :] = jnp.where(hot, 1.0, 0.0).astype(jnp.bfloat16)
    prefix_v[...] = jnp.dot(hot_v[...], upper, preferred_element_type=jnp.float32)
    carry = jnp.zeros((dest_count, 1), jnp.float32)
    for c in range(chunks):
        prefix = prefix_v[c * dest_count : (c + 1) * dest_count, :]
        hot = dest_iota == dest_all[c : c + 1, :]
        rows_v[1, c : c + 1, :] = jnp.sum(jnp.where(hot, prefix + carry, 0.0), axis=0, keepdims=True) - 1.0
        carry = carry + prefix[:, LANES - 1 : LANES]
    pos_v[...] = dest_all * slot_rows + rows_v[1].astype(jnp.int32)
    copy = pltpu.make_async_copy(pos_v, pos_s, sems.at[0])
    copy.start()
    meta_v[...] = jnp.zeros_like(meta_v)
    mrow[...] = jnp.zeros_like(mrow)

    def clear(b, _):
        outf[pl.ds(pl.multiple_of(b * slot_rows, 16), slot_rows), :] = jnp.zeros((slot_rows, LANES), jnp.float32)
        return 0

    lax.fori_loop(0, dest_count, clear, 0)
    fetch.wait()
    copy.wait()
    dest_number = dest_iota.astype(jnp.float32)
    slot_number = lax.broadcasted_iota(jnp.int32, (width, LANES), 0).astype(jnp.float32)

    def move(c, _):
        base = pl.multiple_of(c * LANES, LANES)
        pixf[pl.ds(base, LANES), :] = pix_v[pl.ds(base, LANES), :].astype(jnp.float32)
        dest, rank, weight, local_row, day = (rows_v[v, pl.ds(c, 1), :] for v in range(5))
        hot = dest_number == dest
        place = jnp.where(slot_number == rank, 1.0, 0.0).astype(jnp.bfloat16)
        values = jnp.concatenate([jnp.where(hot, v, 0.0) for v in (weight, local_row, day)], axis=0).astype(jnp.bfloat16)
        meta_v[...] += lax.dot_general(values, place, LAST_LAST, preferred_element_type=jnp.float32)
        for lane in range(LANES):
            outf[pl.ds(pos_s[c, lane], 1), :] = pixf[pl.ds(base + lane, 1), :]
        return 0

    lax.fori_loop(0, chunks, move, 0)
    for v in range(3):
        for i in range(pieces):
            mrow[pl.ds(v * pieces + i, dest_count, stride=META_ROWS), :] = meta_v[
                v * dest_count : (v + 1) * dest_count, i * LANES : (i + 1) * LANES
            ]

    together = 8

    def narrow(i, _):
        for q in range(together):
            b = i * together + q
            at = pl.multiple_of(b * slot_rows, 16)
            first_v[b, :first_rows, :] = outf[pl.ds(at, first_rows), :].astype(jnp.bfloat16)
            first_v[b, first_rows:, :] = mrow[pl.ds(pl.multiple_of(b * META_ROWS, 16), META_ROWS), :].astype(jnp.bfloat16)
            last_v[b] = outf[pl.ds(at + first_rows, slot_rows - first_rows), :].astype(jnp.bfloat16)
        some = pl.ds(i * together, together)
        pltpu.make_async_copy(first_v.at[some], first_ref.at[some], sems.at[1]).start()
        pltpu.make_async_copy(last_v.at[some], last_ref.at[some], sems.at[2]).start()
        return 0

    lax.fori_loop(0, dest_count // together, narrow, 0)
    pltpu.make_async_copy(first_v, first_ref, sems.at[1]).wait()
    pltpu.make_async_copy(last_v, last_ref, sems.at[2]).wait()


def pack(pixels, weights, tile_index, tile_row, granule_day, time_count, space_count, rows_tm, slots):
    swath_rows = pixels.shape[0]
    chunks = swath_rows // LANES
    dest_count = time_count * space_count
    slot_rows, first_rows = split_rows(slots)
    width = round_up(slots, LANES)
    shape = (chunks, LANES)
    first_shape = (dest_count, first_rows + META_ROWS, LANES)
    last_shape = (dest_count, slot_rows - first_rows, LANES)
    return pl.pallas_call(
        functools.partial(pack_kernel, (time_count, space_count, rows_tm, slot_rows, first_rows, width)),
        in_specs=[pl.BlockSpec(memory_space=pltpu.VMEM)] * 4 + [pl.BlockSpec(memory_space=pl.ANY)],
        out_specs=[pl.BlockSpec(memory_space=pl.ANY)] * 2,
        out_shape=[jax.ShapeDtypeStruct(first_shape, jnp.bfloat16), jax.ShapeDtypeStruct(last_shape, jnp.bfloat16)],
        scratch_shapes=[
            pltpu.VMEM(shape, jnp.int32),
            pltpu.SMEM(shape, jnp.int32),
            pltpu.VMEM((5,) + shape, jnp.float32),
            pltpu.VMEM((3 * dest_count, width), jnp.float32),
            pltpu.VMEM((swath_rows, LANES), jnp.float32),
            pltpu.VMEM((dest_count * slot_rows, LANES), jnp.float32),
            pltpu.VMEM((dest_count * META_ROWS, LANES), jnp.float32),
            pltpu.VMEM(first_shape, jnp.bfloat16),
            pltpu.VMEM(last_shape, jnp.bfloat16),
            pltpu.VMEM((swath_rows, LANES), jnp.bfloat16),
            pltpu.VMEM((chunks * dest_count, LANES), jnp.bfloat16),
            pltpu.VMEM((chunks * dest_count, LANES), jnp.float32),
            pltpu.SemaphoreType.DMA((4,)),
        ],
        compiler_params=pltpu.CompilerParams(vmem_limit_bytes=VMEM),
        name="pack",
    )(
        tile_index.reshape(shape),
        tile_row.reshape(shape),
        granule_day.reshape(shape),
        weights.reshape(shape),
        pixels,
    )


def chunks_of(first_slot, rows):
    slot, found = first_slot, []
    while slot < first_slot + rows:
        size = min(32 - slot % 32, first_slot + rows - slot)
        found.append((slot, size))
        slot += size
    return found


def add_rows(total, pixf, code_s, code_row, first_slot, rows, pix_at, count):
    def add_group(row, lane, at):
        places = [code_s[row, lane + u] for u in range(GROUP)]
        made = [total[pl.ds(p, 1), :] + pixf[pl.ds(at + u, 1), :] for u, p in enumerate(places)]
        for p, value in zip(places, made):
            total[pl.ds(p, 1), :] = value

    def add_singly(row, lane, at):
        def one(u, _):
            p = code_s[row, lane + u]
            p = jnp.where(p >= CLASH, p - CLASH, p)
            total[pl.ds(p, 1), :] = total[pl.ds(p, 1), :] + pixf[pl.ds(at + u, 1), :]
            return 0

        lax.fori_loop(0, GROUP, one, 0)

    for slot, chunk in chunks_of(first_slot, rows):
        start = slot - first_slot
        row, lane = code_row(slot // LANES), slot % LANES
        at = pix_at + start
        heads = [code_s[row, lane + g] for g in range(0, chunk, GROUP)]
        clash = functools.reduce(jnp.maximum, heads) >= CLASH

        @pl.when((count > start) & jnp.logical_not(clash))
        def _():
            for g in range(0, chunk, GROUP):
                add_group(row, lane + g, at + g)

        @pl.when((count > start) & clash)
        def _():
            for g, head in zip(range(0, chunk, GROUP), heads):
                pl.when(head < CLASH)(functools.partial(add_group, row, lane + g, at + g))
                pl.when(head >= CLASH)(functools.partial(add_singly, row, lane + g, at + g))


def grid_first_kernel(
    dims, moved_ref, total_ref, code_ref, rest_ref, count_ref, column_ref, meta_v, pixf, code_s, count_s, sems
):
    time_count, space_count, rows_tm, slot_rows, first_rows, width = dims
    day_dev = DAYS // time_count
    blocks = time_count * space_count
    pieces = width // LANES
    spare = rows_tm * DAYS

    meta_v[...] = moved_ref[:, first_rows:, :].astype(jnp.float32).reshape(blocks * META_ROWS, LANES)
    block = lax.broadcasted_iota(jnp.int32, (blocks, LANES), 0)
    offset = jnp.zeros((blocks, LANES), jnp.float32)
    for m in range(1, time_count):
        offset = offset + jnp.where(block >= m * space_count, float(day_dev), 0.0)
    within = lax.broadcasted_iota(jnp.int32, (blocks, LANES), 1) % GROUP
    count = jnp.zeros((blocks, 1), jnp.float32)
    for i in range(pieces):
        weight, local_row, day = (meta_v[pl.ds(v * pieces + i, blocks, stride=META_ROWS), :] for v in range(3))
        used = weight > 0.0
        count = count + jnp.sum(jnp.where(used, 1.0, 0.0), axis=1, keepdims=True)
        column_ref[i * LANES : (i + 1) * LANES, :] = jnp.transpose(weight)
        code = jnp.where(used, local_row * DAYS + (day + offset), float(spare)).astype(jnp.int32)
        clash = jnp.zeros(code.shape, jnp.int32)
        for k in range(1, GROUP):
            ahead = pltpu.roll(code, LANES - k, 1)
            clash = jnp.where((ahead == code) & (within + k < GROUP) & (code < spare), 1, clash)
        k = 1
        while k < GROUP:
            ahead = pltpu.roll(clash, LANES - k, 1)
            clash = jnp.where(within + k < GROUP, jnp.maximum(clash, ahead), clash)
            k *= 2
        code_ref[i * blocks : (i + 1) * blocks, :] = jnp.where((within == 0) & (clash > 0), code + CLASH, code)
    rest_ref[...] = code_ref[first_rows // LANES * blocks :, :]
    count_ref[...] = jnp.broadcast_to(count, (blocks, LANES)).astype(jnp.int32)
    code_copy = pltpu.make_async_copy(code_ref, code_s, sems.at[0])
    count_copy = pltpu.make_async_copy(count_ref, count_s, sems.at[1])
    code_copy.start()
    count_copy.start()

    for b in range(blocks):
        column = column_ref[:first_rows, b : b + 1]
        pixf[b * first_rows : (b + 1) * first_rows, :] = moved_ref[b, :first_rows, :].astype(jnp.float32) * column

    def clear(i, _):
        total_ref[pl.ds(pl.multiple_of(i * DAYS, DAYS), DAYS), :] = jnp.zeros((DAYS, LANES), jnp.float32)
        return 0

    lax.fori_loop(0, rows_tm, clear, 0)
    total_ref[spare:, :] = jnp.zeros((8, LANES), jnp.float32)
    code_copy.wait()
    count_copy.wait()

    def add(b, _):
        add_rows(total_ref, pixf, code_s, lambda i: i * blocks + b, 0, first_rows, b * first_rows, count_s[b, 0])
        return 0

    lax.fori_loop(0, blocks, add, 0)


def grid_last_kernel(
    dims, code_s, count_s, column_ref, moved_ref, first_ref, field_ref, keep_ref, give_ref,
    total, first_v, moved_v, pixf, field_v, gram_v, first_sems, block_sems, out_sem
):
    time_count, space_count, rows_tm, slot_rows, first_rows, width = dims
    blocks = time_count * space_count
    last_rows = slot_rows - first_rows
    group = rows_tm // STEPS
    skipped = first_rows // LANES

    def load(i):
        at = pl.ds(pl.multiple_of(i * group * DAYS, DAYS), group * DAYS)
        return pltpu.make_async_copy(first_ref.at[at], first_v.at[at], first_sems.at[i])

    def fetch(b):
        return pltpu.make_async_copy(moved_ref.at[b], moved_v.at[b], block_sems.at[b])

    for b in range(blocks):
        pl.when(count_s[b, 0] > first_rows)(fetch(b).start)
    for i in range(STEPS):
        load(i).start()

    def clear(i, _):
        total[pl.ds(pl.multiple_of(i * DAYS, DAYS), DAYS), :] = jnp.zeros((DAYS, LANES), jnp.float32)
        return 0

    lax.fori_loop(0, rows_tm, clear, 0)
    total[rows_tm * DAYS :, :] = jnp.zeros((8, LANES), jnp.float32)
    for b in range(blocks):

        @pl.when(count_s[b, 0] > first_rows)
        def _():
            fetch(b).wait()
            column = column_ref[first_rows:slot_rows, b : b + 1]
            pixf[b * last_rows : (b + 1) * last_rows, :] = moved_v[b].astype(jnp.float32) * column

    def add(b, _):
        rest = count_s[b, 0] - first_rows

        @pl.when(rest > 0)
        def _():
            add_rows(
                total, pixf, code_s, lambda i: (i - skipped) * blocks + b, first_rows, last_rows, b * last_rows, rest
            )

        return 0

    lax.fori_loop(0, blocks, add, 0)

    def send(i):
        at = pl.ds(i * group, group)
        return pltpu.make_async_copy(field_v.at[at], field_ref.at[at], out_sem)

    def settle(i):
        for q in range(i * group, (i + 1) * group):
            at = pl.ds(q * DAYS, DAYS)
            field_v[q] = (first_v[at, :] + total[at, :]).astype(jnp.bfloat16)

    def multiply(i):
        both = jnp.concatenate([field_v[q] for q in range(i * group, (i + 1) * group)], axis=1)
        part = lax.dot_general(both[:RANK], both, LAST_LAST, preferred_element_type=jnp.float32)
        for c in range(DAYS // LANES):
            here = part[:, c * LANES : (c + 1) * LANES]
            gram_v[c] = here if i == 0 else gram_v[c] + here

    for i in range(STEPS):
        load(i).wait()
        settle(i)
        if i > 0:
            send(i - 1).start()
            multiply(i - 1)
    send(STEPS - 1).start()
    multiply(STEPS - 1)
    odd = lax.axis_index("tm") % 2
    half = DAYS // LANES // 2
    for c in range(half):
        keep_ref[c] = gram_v[odd * half + c]
        give_ref[c] = gram_v[(1 - odd) * half + c]
    pltpu.make_async_copy(field_v, field_ref, out_sem).wait()


def grid_rows(moved_first, moved_last, time_count, space_count, rows_tm, slots):
    slot_rows, first_rows = split_rows(slots)
    last_rows = slot_rows - first_rows
    width = round_up(slots, LANES)
    blocks = time_count * space_count
    dims = (time_count, space_count, rows_tm, slot_rows, first_rows, width)
    codes = (blocks * width // LANES, LANES)
    rest = (codes[0] - first_rows // LANES * blocks, LANES)
    counts = (blocks, LANES)
    columns = (width, blocks)
    sums = (rows_tm * DAYS + 8, LANES)
    half = (DAYS // LANES // 2, RANK, LANES)
    params = pltpu.CompilerParams(vmem_limit_bytes=VMEM)
    moved_first, moved_last = (pltpu.with_memory_space_constraint(v, pltpu.VMEM) for v in (moved_first, moved_last))
    total, _, code, count, column = pl.pallas_call(
        functools.partial(grid_first_kernel, dims),
        out_shape=[
            jax.ShapeDtypeStruct(sums, jnp.float32),
            jax.ShapeDtypeStruct(codes, jnp.int32),
            jax.ShapeDtypeStruct(rest, jnp.int32),
            jax.ShapeDtypeStruct(counts, jnp.int32),
            jax.ShapeDtypeStruct(columns, jnp.float32),
        ],
        scratch_shapes=[
            pltpu.VMEM((blocks * META_ROWS, LANES), jnp.float32),
            pltpu.VMEM((blocks * first_rows, LANES), jnp.float32),
            pltpu.SMEM(codes, jnp.int32),
            pltpu.SMEM(counts, jnp.int32),
            pltpu.SemaphoreType.DMA((2,)),
        ],
        compiler_params=params,
        cost_estimate=pl.CostEstimate(flops=0, bytes_accessed=60_000_000, transcendentals=0),
        name="grid_first",
    )(moved_first)
    whole = pl.BlockSpec(memory_space=pltpu.VMEM)
    return pl.pallas_call(
        functools.partial(grid_last_kernel, dims),
        in_specs=[
            pl.BlockSpec(memory_space=pltpu.SMEM),
            pl.BlockSpec(memory_space=pltpu.SMEM),
            whole,
            pl.BlockSpec(memory_space=pl.ANY),
            pl.BlockSpec(memory_space=pl.ANY),
        ],
        out_specs=[pl.BlockSpec(memory_space=pl.ANY), whole, whole],
        out_shape=[
            jax.ShapeDtypeStruct((rows_tm, DAYS, LANES), jnp.bfloat16),
            pltpu.VMEM(half, jnp.float32),
            pltpu.VMEM(half, jnp.float32),
        ],
        scratch_shapes=[
            pltpu.VMEM(sums, jnp.float32),
            pltpu.VMEM((rows_tm * DAYS, LANES), jnp.float32),
            pltpu.VMEM((blocks, last_rows, LANES), jnp.bfloat16),
            pltpu.VMEM((blocks * last_rows, LANES), jnp.float32),
            pltpu.VMEM((rows_tm, DAYS, LANES), jnp.bfloat16),
            pltpu.VMEM((DAYS // LANES, RANK, LANES), jnp.float32),
            pltpu.SemaphoreType.DMA((STEPS,)),
            pltpu.SemaphoreType.DMA((blocks,)),
            pltpu.SemaphoreType.DMA,
        ],
        compiler_params=params,
        name="grid_last_and_gram",
    )(code, count, column, moved_last, total)


def dot_f32(a, b, dims=(((1,), (0,)), ((), ()))):
    return lax.dot_general(a, b, dims, precision=lax.Precision.HIGHEST, preferred_element_type=jnp.float32)


def dot_three(a, b, dims=(((1,), (0,)), ((), ()))):
    a_high, b_high = a.astype(jnp.bfloat16), b.astype(jnp.bfloat16)
    a_low = (a - a_high.astype(jnp.float32)).astype(jnp.bfloat16)
    b_low = (b - b_high.astype(jnp.float32)).astype(jnp.bfloat16)
    left, right = dims[0][0][0], dims[0][1][0]
    a_all = jnp.concatenate([a_high, a_high, a_low], axis=left)
    b_all = jnp.concatenate([b_high, b_low, b_high], axis=right)
    return lax.dot_general(a_all, b_all, dims, preferred_element_type=jnp.float32)


def invert(x):
    guess = pl.reciprocal(x, approx=True)
    guess = guess * (2.0 - x * guess)
    return guess * (2.0 - x * guess)


def lower_inverse(a):
    n = a.shape[0]
    full = (8, n)
    tiles = [a[8 * i : 8 * i + 8, :] for i in range(n // 8)]
    lane = lax.broadcasted_iota(jnp.int32, full, 1)
    down = lax.broadcasted_iota(jnp.int32, full, 0)
    out = []
    for t in range(n // 8):
        k = 8 * t
        block = (lane >= k) & (lane < k + 8)
        panel = tiles[t]
        cols = [jnp.broadcast_to(panel[:, k + c : k + c + 1], full) for c in range(8)]
        e = {(i, c): jnp.broadcast_to(cols[c][i : i + 1, :], full) for c in range(8) for i in range(c, 8)}
        start = jnp.where(block, jnp.where(lane == k + down, 1.0, 0.0), panel)
        rows = [jnp.broadcast_to(start[i : i + 1, :], full) for i in range(8)]
        held = []
        for s in range(0, 8, 2):
            p, q, r = e[s, s], e[s + 1, s], e[s + 1, s + 1]
            det = p * r - q * q
            inv = invert(det)
            factors = {}
            for i in range(s + 2, 8):
                x, y = e[i, s], e[i, s + 1]
                factors[i] = (r * x - q * y, p * y - q * x)
            for i in range(s + 2, 8):
                u, v = factors[i]
                for c in range(s + 2, i + 1):
                    e[i, c] = e[i, c] - (u * e[c, s] + v * e[c, s + 1]) * inv
                rows[i] = rows[i] - (u * rows[s] + v * rows[s + 1]) * inv
            held.append((p, q, r, det, inv, factors))
        done = jnp.zeros(full, jnp.float32)
        solved = [None] * 8
        for s in (6, 4, 2, 0):
            p, q, r, det, inv, factors = held[s // 2]
            root = lax.rsqrt(p)
            done = jnp.where(down == s, rows[s] * root, done)
            done = jnp.where(down == s + 1, (rows[s + 1] * p - q * rows[s]) * (root * lax.rsqrt(det)), done)
            first, second = r * rows[s] - q * rows[s + 1], p * rows[s + 1] - q * rows[s]
            for i in range(7, s + 1, -1):
                u, v = factors[i]
                first, second = first - u * solved[i], second - v * solved[i]
            solved[s], solved[s + 1] = first * inv, second * inv
        out.append(jnp.where(lane < k + 8, done, 0.0))
        for i in range(t + 1, n // 8):
            terms = [jnp.broadcast_to(tiles[i][:, k + c : k + c + 1], full) * solved[c] for c in range(8)]
            while len(terms) > 1:
                terms = [terms[j] + terms[j + 1] for j in range(0, len(terms), 2)]
            tiles[i] = jnp.where(block, 0.0, tiles[i]) - terms[0]
    return jnp.concatenate(out, axis=0)


def solve_kernel(scale, own_ref, other_ref, field_ref, basis_ref, prop_ref, gram_v, field_v, basis_v, sems):
    h = LANES
    pieces = DAYS // h
    rows_here = field_v.shape[0]
    load = pltpu.make_async_copy(field_ref.at[:, pl.ds(0, RANK), :], field_v, sems.at[0])
    load.start()
    odd = lax.axis_index("tm") % 2
    for c in range(pieces // 2):
        gram_v[odd * (pieces // 2) + c] = own_ref[c]
        gram_v[(1 - odd) * (pieces // 2) + c] = other_ref[c]

    gram = jnp.concatenate([gram_v[i] for i in range(pieces)], axis=1)
    eye = lax.broadcasted_iota(jnp.int32, (h, h), 0) == lax.broadcasted_iota(jnp.int32, (h, h), 1)
    a11, a12, a22 = gram_v[0, :h, :], gram_v[1, :h, :], gram_v[1, h:, :]
    size_col, size_row = [], []
    for part in (a11, a22):
        diag = jnp.where(eye, part, 0.0)
        size_col.append(lax.rsqrt(jnp.sum(diag, axis=1, keepdims=True)))
        size_row.append(lax.rsqrt(jnp.sum(diag, axis=0, keepdims=True)))
    top, low = gram[:h], gram[h:]
    x1 = lower_inverse(a11 * size_col[0] * size_row[0])
    r12 = dot_f32(x1, a12 * size_col[0] * size_row[1])
    x2 = lower_inverse(a22 * size_col[1] * size_row[1] - dot_f32(r12, r12, FIRST_FIRST))
    factor_top = dot_f32(x1, top * size_col[0])
    schur = low[:, h:] * size_col[1] - dot_f32(r12, factor_top[:, h:], FIRST_FIRST)
    mixed = -dot_f32(x2, dot_f32(r12, x1, FIRST_FIRST))
    factor_low = dot_f32(x2, schur)
    lower = jnp.concatenate(
        [
            jnp.concatenate([x1 * size_row[0], jnp.zeros((h, h), jnp.float32)], axis=1),
            jnp.concatenate([mixed * size_row[0], x2 * size_row[1]], axis=1),
        ],
        axis=0,
    )
    inverse = (scale * lower).astype(jnp.bfloat16)
    load.wait()

    def project(i):
        both = jnp.concatenate([field_v[2 * i], field_v[2 * i + 1]], axis=1)
        made = jnp.dot(inverse, both, preferred_element_type=jnp.float32).astype(jnp.bfloat16)
        basis_v[2 * i] = made[:, :h]
        basis_v[2 * i + 1] = made[:, h:]

    down = lax.broadcasted_iota(jnp.int32, (RANK, DAYS), 0)
    across = lax.broadcasted_iota(jnp.int32, (RANK, DAYS), 1)
    factor = jnp.concatenate(
        [factor_top, jnp.concatenate([jnp.zeros((h, h), jnp.float32), factor_low], axis=1)], axis=0
    )
    factor = jnp.where(across >= down, factor, 0.0)
    ahead = jnp.where(across < DAYS - 1, pltpu.roll(factor, DAYS - 1, 1), 0.0)
    cross = dot_three(ahead, factor, LAST_LAST)
    polar = cross / jnp.sqrt(jnp.sum(cross * cross) + 1e-06)
    todo = list(range(rows_here // 2))
    share = -(-len(todo) // (ITERS - 1))
    store = pltpu.make_async_copy(basis_v, basis_ref, sems.at[1])
    for n in range(ITERS):
        square = dot_three(polar, polar, LAST_LAST)
        for i in todo[n * share : (n + 1) * share]:
            project(i)
        if n == ITERS - 2:
            store.start()
        polar = 1.5 * polar - 0.5 * dot_three(square, polar)
    prop_ref[...] = math.sqrt(RANK) * polar
    store.wait()


def solve(own, other, field, cell_total):
    rows_tm = field.shape[0]
    part = (rows_tm, RANK, LANES)
    whole = pl.BlockSpec(memory_space=pltpu.VMEM)
    own, other = (pltpu.with_memory_space_constraint(v, pltpu.VMEM) for v in (own, other))
    return pl.pallas_call(
        functools.partial(solve_kernel, math.sqrt(cell_total)),
        in_specs=[whole, whole, pl.BlockSpec(memory_space=pl.ANY)],
        out_specs=[pl.BlockSpec(memory_space=pl.ANY), whole],
        out_shape=[
            jax.ShapeDtypeStruct(part, jnp.bfloat16),
            jax.ShapeDtypeStruct((RANK, RANK), jnp.float32),
        ],
        scratch_shapes=[
            pltpu.VMEM((DAYS // LANES, RANK, LANES), jnp.float32),
            pltpu.VMEM(part, jnp.bfloat16),
            pltpu.VMEM(part, jnp.bfloat16),
            pltpu.SemaphoreType.DMA((2,)),
        ],
        compiler_params=pltpu.CompilerParams(vmem_limit_bytes=VMEM),
        name="factor_basis_and_polar",
    )(own, other, field)


def body(pixels, weights, tile_index, tile_row, granule_day):
    swath_rows = pixels.shape[0]
    width = pixels.shape[1]
    space_count = lax.axis_size("space")
    time_count = lax.axis_size("tm")
    dest_count = time_count * space_count
    rows_tm = GR_DEV // time_count
    slots = 2 * swath_rows // space_count // time_count
    axes = ("tm", "space")
    first, last = pack(pixels, weights, tile_index, tile_row, granule_day, time_count, space_count, rows_tm, slots)
    first = lax.all_to_all(first, axes, split_axis=0, concat_axis=0, tiled=True)
    last = lax.all_to_all(last, axes, split_axis=0, concat_axis=0, tiled=True)
    field, keep, give = grid_rows(first, last, time_count, space_count, rows_tm, slots)

    swap = [(t, t ^ 1) for t in range(time_count)]
    peers = [[t * space_count + s for t in range(core, time_count, 2) for s in range(space_count)] for core in (0, 1)]
    among = functools.partial(
        lax.all_to_all, axis_name=axes, split_axis=0, concat_axis=0, axis_index_groups=peers, tiled=True
    )
    pieces = (keep + lax.ppermute(give, "tm", swap)).reshape(dest_count // 2, -1, LANES)
    mine = jnp.sum(among(pieces), axis=0, keepdims=True)
    own = among(jnp.broadcast_to(mine, pieces.shape)).reshape(keep.shape)
    other = lax.ppermute(own, "tm", swap)
    cell_total = space_count * GR_DEV * width
    basis, propagator = solve(own, other, field, cell_total)
    return (field[None], basis[None], propagator)


def solution(mesh):
    placed = (
        P(("tm", "space"), None),
        P(("tm", "space")),
        P(("tm", "space")),
        P(("tm", "space")),
        P(("tm", "space")),
    )
    return jax.shard_map(
        body,
        mesh=mesh,
        in_specs=placed,
        out_specs=(P("space", "tm", None, None), P("space", "tm", None, None), P()),
        check_vma=False,
    )
```

profile of v0, /device:TPU:0, one launch (start us, length us, event | category | flops | bytes accessed | tf_op | source)
XLA Modules:
  0.0 149.7 jit_solution(1258021619457079653)
XLA Ops:
  0.6 11.3 %pack.1 = (bf16[32,224,128]{2,1,0:T(8,128)(2,1)}, bf16[32,112,128]{2,1,0:T(8,128)(2,1)}) custom-call(s32[40,128]{1,0:T(8,128)} %bitcast.12, s32[40,128]{1,0:T(8,128)} %bitcast.13, s32[40,128]{1,0:T(8,128)} %bitcast.14, bf16[40,128]{1,0:T(8,128)(2,1)} %bitcast.15, bf16[5120,128]{1,0:T(8,128)(2,1)} %pix_ref.1), custom_call_target="tpu_custom_call" | custom-call | tf_op jit(solution)/shard_map/pack/pallas_call | solution.py:134
  11.9 51.8 %all_to_all.20.moved_ref = bf16[32,224,128]{2,1,0:T(8,128)(2,1)S(1)} all-to-all(bf16[32,224,128]{2,1,0:T(8,128)(2,1)} %get-tuple-element.14), channel_id=1, replica_groups=mesh['tm'=4,'space'=8] {'tm','space'}, dimensions={0} | all-to-all | bytes 3670016 | tf_op jit(solution)/shard_map/all_to_all | solution.py:586
  63.7 2.6 %all-to-all-start.1 = ((bf16[32,112,128]{2,1,0:T(8,128)(2,1)}), bf16[32,112,128]{2,1,0:T(8,128)(2,1)S(1)}, u32[]{:S(2)}, u32[]{:S(2)}) async-start(bf16[32,112,128]{2,1,0:T(8,128)(2,1)} %get-tuple-element.18), calls=%async_computation.1 | async-start | bytes 1835008 | tf_op jit(solution)/shard_map/all_to_all | solution.py:587
  66.3 18.3 %grid_first.1 = (f32[20488,128]{1,0:T(8,128)}, s32[96,128]{1,0:T(8,128)}, s32[64,128]{1,0:T(8,128)}, s32[32,128]{1,0:T(8,128)}, f32[384,32]{1,0:T(8,128)}) custom-call(bf16[32,224,128]{2,1,0:T(8,128)(2,1)S(1)} %all_to_all.20.moved_ref), custom_call_target="tpu_custom_call" | custom-call | bytes 60000000 | tf_op jit(solution)/shard_map/grid_first/pallas_call | solution.py:363
  84.6 6.5 %all-to-all-done.1.moved_ref = bf16[32,112,128]{2,1,0:T(8,128)(2,1)S(1)} async-done(((bf16[32,112,128]{2,1,0:T(8,128)(2,1)}), bf16[32,112,128]{2,1,0:T(8,128)(2,1)S(1)}, u32[]{:S(2)}, u32[]{:S(2)}) %all-to-all-start.1) | async-done | bytes 917536 | tf_op jit(solution)/shard_map/all_to_all | solution.py:587
  91.1 8.3 %grid_last_and_gram.1 = (bf16[40,512,128]{2,1,0:T(8,128)(2,1)}, f32[2,256,128]{2,1,0:T(8,128)S(1)}, f32[2,256,128]{2,1,0:T(8,128)S(1)}) custom-call(s32[64,128]{1,0:T(8,128)} %get-tuple-element.15.code_s, s32[32,128]{1,0:T(8,128)} %get-tuple-element.16.count_s, f32[384,32]{1,0:T(8,128)} %get-tuple-element.17.column_ref, ...), custom_call_target="tpu_custom_call" | custom-call | tf_op jit(solution)/shard_map/grid_last_and_gram/pallas_call | solution.py:384
  99.4 0.1 collective-permute-start
  99.5 1.5 %collective-permute-done = f32[2,256,128]{2,1,0:T(8,128)S(1)} collective-permute-done((f32[2,256,128]{2,1,0:T(8,128)S(1)}, f32[2,256,128]{2,1,0:T(8,128)S(1)}, u32[]{:S(2)}, u32[]{:S(2)}) %collective-permute-start) | collective-permute-done | bytes 262176 | tf_op jit(solution)/shard_map/ppermute | solution.py:595
  101.0 14.9 %all_to_all.21 = f32[16,32,128]{2,1,0:T(8,128)S(1)} all-to-all(f32[16,32,128]{2,1,0:T(8,128)S(1)} %bitcast.11), channel_id=1, replica_groups={{0,1,2,3,4,5,6,7,16,17,18,19,20,21,22,23},{8,9,10,11,12,13,14,15,24,25,..., dimensions={0} | all-to-all | bytes 524288 | tf_op jit(solution)/shard_map/all_to_all | solution.py:596
  116.0 12.6 %all_to_all.22 = f32[16,32,128]{2,1,0:T(8,128)S(1)} all-to-all(f32[16,32,128]{2,1,0:T(8,128)S(1)} %broadcast_in_dim.13), channel_id=1, replica_groups={{0,1,2,3,4,5,6,7,16,17,18,19,20,21,22,23},{8,9,10,11,12,13,14,15,24,25,..., dimensions={0} | all-to-all | bytes 524288 | tf_op jit(solution)/shard_map/all_to_all | solution.py:597
  128.5 0.0 collective-permute-start.1
  128.5 1.5 %collective-permute-done.1.other_ref = f32[2,256,128]{2,1,0:T(8,128)S(1)} collective-permute-done((f32[2,256,128]{2,1,0:T(8,128)S(1)}, f32[2,256,128]{2,1,0:T(8,128)S(1)}, u32[]{:S(2)}, u32[]{:S(2)}) %collective-permute-start.1) | collective-permute-done | bytes 262176 | tf_op jit(solution)/shard_map/ppermute | solution.py:598
  130.1 19.5 %factor_basis_and_polar.1 = (bf16[40,256,128]{2,1,0:T(8,128)(2,1)}, f32[256,256]{1,0:T(8,128)}) custom-call(f32[2,256,128]{2,1,0:T(8,128)S(1)} %bitcast.9, f32[2,256,128]{2,1,0:T(8,128)S(1)} %collective-permute-done.1.other_ref, bf16[40,512,128]{2,1,0:T(8,128)(2,1)} %get-tuple-element.20.field_ref), custom_call_target="tpu_custom_call" | custom-call | tf_op jit(solution)/shard_map/factor_basis_and_polar/pallas_call | solution.py:557
  (3 shorter events, 0.1 us)
Async XLA Ops:
  63.7 27.4 %all-to-all-start.1 = ((bf16[32,112,128]{2,1,0:T(8,128)(2,1)}), bf16[32,112,128]{2,1,0:T(8,128)(2,1)S(1)}, u32[]{:S(2)}, u32[]{:S(2)}) async-start(bf16[32,112,128]{2,1,0:T(8,128)(2,1)} %get-tuple-element.18), calls=%async_computation.1 | async-start | bytes 1835008 | tf_op jit(solution)/shard_map/all_to_all | solution.py:587
  99.4 1.6 %collective-permute-start = (f32[2,256,128]{2,1,0:T(8,128)S(1)}, f32[2,256,128]{2,1,0:T(8,128)S(1)}, u32[]{:S(2)}, u32[]{:S(2)}) collective-permute-start(f32[2,256,128]{2,1,0:T(8,128)S(1)} %get-tuple-element.22), channel_id=1, source_target_pairs={{0,8},{8,0},{16,24},{24,16},{1,9},{9,1},{17,25},{25,17},{2,10},{10... | collective-permute-start | bytes 786440 | tf_op jit(solution)/shard_map/ppermute | solution.py:595
  128.5 1.5 %collective-permute-start.1 = (f32[2,256,128]{2,1,0:T(8,128)S(1)}, f32[2,256,128]{2,1,0:T(8,128)S(1)}, u32[]{:S(2)}, u32[]{:S(2)}) collective-permute-start(f32[2,256,128]{2,1,0:T(8,128)S(1)} %bitcast.8), channel_id=1, source_target_pairs={{0,8},{8,0},{16,24},{24,16},{1,9},{9,1},{17,25},{25,17},{2,10},{10... | collective-permute-start | bytes 786440 | tf_op jit(solution)/shard_map/ppermute | solution.py:598
where the time goes:
time: 150 us
  blocking collectives  79.2 us (53%)
  Pallas kernels  57.3 us (38%)
  waiting for transfers between devices  9.57 us (6%)
  starting transfers between devices  2.71 us (2%)
    all_to_all x1, blocking collectives, body(): first = lax.all_to_all(first, axes, split_axis=0, concat_axis=0, tiled=True)  51.8 us
    pallas_call x1, Pallas kernels, solve(): pl.pallas_call(functools.partial(solve_kernel, math.sqrt(cell_total)), in...  19.5 us
    pallas_call x1, Pallas kernels, grid_rows(): pl.pallas_call(functools.partial(grid_first_kernel, dims), out_shape=[jax...  18.3 us
    all_to_all x1, blocking collectives, body(): mine = jnp.sum(among(pieces), axis=0, keepdims=True)  14.9 us
    all_to_all x1, blocking collectives, body(): own = among(jnp.broadcast_to(mine, pieces.shape)).reshape(keep.shape)  12.6 us
    pallas_call x1, Pallas kernels, pack(): pl.pallas_call(functools.partial(pack_kernel, (time_count, space_count, r...  11.3 us
    pallas_call x1, Pallas kernels, grid_rows(): pl.pallas_call(functools.partial(grid_last_kernel, dims), in_specs=[pl.Bl...  8.27 us
    all_to_all x1, waiting for transfers between devices, body(): last = lax.all_to_all(last, axes, split_axis=0, concat_axis=0, tiled=True)  6.52 us
  transfers between devices with their start and end apart: 3, of which 3 were waited for; matrix products, arithmetic and copies ran while one was open for 0% of the time, Pallas kernels for 12%

commit v1 on v0

--- a/solution.py
+++ b/solution.py
@@ -13,7 +13,6 @@
 RANK = 256
 ITERS = 8
 LANES = 128
-META_ROWS = 16
 GROUP = 16
 CLASH = 1 << 20
 STEPS = 5
@@ -32,11 +31,17 @@
     return rows, rows * 13 // 20 // 16 * 16
 
 
+def meta_layout(slots):
+    pieces = round_up(slots, LANES) // LANES
+    folded = 3 * pieces > 8 and 3 * pieces - 1 <= 8 and slots % LANES <= LANES // 2
+    return (8 if folded else round_up(3 * pieces, 8)), folded
+
+
 def pack_kernel(
     dims, tile_ref, row_ref, day_ref, weight_ref, pix_ref, first_ref, last_ref, pos_v, pos_s, rows_v, meta_v, pixf, outf, mrow,
     first_v, last_v, pix_v, hot_v, prefix_v, sems
 ):
-    time_count, space_count, rows_tm, slot_rows, first_rows, width = dims
+    time_count, space_count, rows_tm, slot_rows, first_rows, width, (meta_rows, folded) = dims
     dest_count = time_count * space_count
     chunks = tile_ref.shape[0]
     pieces = width // LANES
@@ -81,27 +86,40 @@
     lax.fori_loop(0, dest_count, clear, 0)
     fetch.wait()
     copy.wait()
-    dest_number = dest_iota.astype(jnp.float32)
-    slot_number = lax.broadcasted_iota(jnp.int32, (width, LANES), 0).astype(jnp.float32)
+    both = 2 * LANES
+    dest_number = lax.broadcasted_iota(jnp.int32, (dest_count, both), 0).astype(jnp.float32)
+    slot_number = lax.broadcasted_iota(jnp.int32, (width, both), 0).astype(jnp.float32)
 
     def move(c, _):
-        base = pl.multiple_of(c * LANES, LANES)
-        pixf[pl.ds(base, LANES), :] = pix_v[pl.ds(base, LANES), :].astype(jnp.float32)
-        dest, rank, weight, local_row, day = (rows_v[v, pl.ds(c, 1), :] for v in range(5))
+        base = pl.multiple_of(c * both, both)
+        pixf[pl.ds(base, both), :] = pix_v[pl.ds(base, both), :].astype(jnp.float32)
+        dest, rank, weight, local_row, day = (
+            jnp.concatenate([rows_v[v, pl.ds(2 * c, 1), :], rows_v[v, pl.ds(2 * c + 1, 1), :]], axis=1) for v in range(5)
+        )
         hot = dest_number == dest
         place = jnp.where(slot_number == rank, 1.0, 0.0).astype(jnp.bfloat16)
         values = jnp.concatenate([jnp.where(hot, v, 0.0) for v in (weight, local_row, day)], axis=0).astype(jnp.bfloat16)
         meta_v[...] += lax.dot_general(values, place, LAST_LAST, preferred_element_type=jnp.float32)
-        for lane in range(LANES):
-            outf[pl.ds(pos_s[c, lane], 1), :] = pixf[pl.ds(base + lane, 1), :]
+        for half in range(2):
+            for lane in range(LANES):
+                outf[pl.ds(pos_s[2 * c + half, lane], 1), :] = pixf[pl.ds(base + half * LANES + lane, 1), :]
         return 0
 
-    lax.fori_loop(0, chunks, move, 0)
+    lax.fori_loop(0, chunks // 2, move, 0)
+    whole = pieces - 1 if folded else pieces
+
+    def lanes(v, i):
+        return meta_v[v * dest_count : (v + 1) * dest_count, i * LANES : (i + 1) * LANES]
+
+    def put(at, value):
+        mrow[pl.ds(at, dest_count, stride=meta_rows), :] = value
+
     for v in range(3):
-        for i in range(pieces):
-            mrow[pl.ds(v * pieces + i, dest_count, stride=META_ROWS), :] = meta_v[
-                v * dest_count : (v + 1) * dest_count, i * LANES : (i + 1) * LANES
-            ]
+        for i in range(whole):
+            put(v * whole + i, lanes(v, i))
+    if folded:
+        put(3 * whole, lanes(0, whole) + pltpu.roll(lanes(1, whole), LANES // 2, 1))
+        put(3 * whole + 1, lanes(2, whole))
 
     together = 8
 
@@ -110,7 +128,7 @@
             b = i * together + q
             at = pl.multiple_of(b * slot_rows, 16)
             first_v[b, :first_rows, :] = outf[pl.ds(at, first_rows), :].astype(jnp.bfloat16)
-            first_v[b, first_rows:, :] = mrow[pl.ds(pl.multiple_of(b * META_ROWS, 16), META_ROWS), :].astype(jnp.bfloat16)
+            first_v[b, first_rows:, :] = mrow[pl.ds(pl.multiple_of(b * meta_rows, 8), meta_rows), :].astype(jnp.bfloat16)
             last_v[b] = outf[pl.ds(at + first_rows, slot_rows - first_rows), :].astype(jnp.bfloat16)
         some = pl.ds(i * together, together)
         pltpu.make_async_copy(first_v.at[some], first_ref.at[some], sems.at[1]).start()
@@ -129,10 +147,11 @@
     slot_rows, first_rows = split_rows(slots)
     width = round_up(slots, LANES)
     shape = (chunks, LANES)
-    first_shape = (dest_count, first_rows + META_ROWS, LANES)
+    layout = meta_layout(slots)
+    first_shape = (dest_count, first_rows + layout[0], LANES)
     last_shape = (dest_count, slot_rows - first_rows, LANES)
     return pl.pallas_call(
-        functools.partial(pack_kernel, (time_count, space_count, rows_tm, slot_rows, first_rows, width)),
+        functools.partial(pack_kernel, (time_count, space_count, rows_tm, slot_rows, first_rows, width, layout)),
         in_specs=[pl.BlockSpec(memory_space=pltpu.VMEM)] * 4 + [pl.BlockSpec(memory_space=pl.ANY)],
         out_specs=[pl.BlockSpec(memory_space=pl.ANY)] * 2,
         out_shape=[jax.ShapeDtypeStruct(first_shape, jnp.bfloat16), jax.ShapeDtypeStruct(last_shape, jnp.bfloat16)],
@@ -143,7 +162,7 @@
             pltpu.VMEM((3 * dest_count, width), jnp.float32),
             pltpu.VMEM((swath_rows, LANES), jnp.float32),
             pltpu.VMEM((dest_count * slot_rows, LANES), jnp.float32),
-            pltpu.VMEM((dest_count * META_ROWS, LANES), jnp.float32),
+            pltpu.VMEM((dest_count * layout[0], LANES), jnp.float32),
             pltpu.VMEM(first_shape, jnp.bfloat16),
             pltpu.VMEM(last_shape, jnp.bfloat16),
             pltpu.VMEM((swath_rows, LANES), jnp.bfloat16),
@@ -209,13 +228,22 @@
 def grid_first_kernel(
     dims, moved_ref, total_ref, code_ref, rest_ref, count_ref, column_ref, meta_v, pixf, code_s, count_s, sems
 ):
-    time_count, space_count, rows_tm, slot_rows, first_rows, width = dims
+    time_count, space_count, rows_tm, slot_rows, first_rows, width, (meta_rows, folded) = dims
     day_dev = DAYS // time_count
     blocks = time_count * space_count
     pieces = width // LANES
     spare = rows_tm * DAYS
 
-    meta_v[...] = moved_ref[:, first_rows:, :].astype(jnp.float32).reshape(blocks * META_ROWS, LANES)
+    meta_v[...] = moved_ref[:, first_rows:, :].astype(jnp.float32).reshape(blocks * meta_rows, LANES)
+    whole = pieces - 1 if folded else pieces
+    early = lax.broadcasted_iota(jnp.int32, (blocks, LANES), 1) < LANES // 2
+
+    def lanes(v, i):
+        if i < whole:
+            return meta_v[pl.ds(v * whole + i, blocks, stride=meta_rows), :]
+        tail = meta_v[pl.ds(3 * whole + v // 2, blocks, stride=meta_rows), :]
+        return jnp.where(early, pltpu.roll(tail, LANES // 2, 1) if v == 1 else tail, 0.0)
+
     block = lax.broadcasted_iota(jnp.int32, (blocks, LANES), 0)
     offset = jnp.zeros((blocks, LANES), jnp.float32)
     for m in range(1, time_count):
@@ -223,7 +251,7 @@
     within = lax.broadcasted_iota(jnp.int32, (blocks, LANES), 1) % GROUP
     count = jnp.zeros((blocks, 1), jnp.float32)
     for i in range(pieces):
-        weight, local_row, day = (meta_v[pl.ds(v * pieces + i, blocks, stride=META_ROWS), :] for v in range(3))
+        weight, local_row, day = (lanes(v, i) for v in range(3))
         used = weight > 0.0
         count = count + jnp.sum(jnp.where(used, 1.0, 0.0), axis=1, keepdims=True)
         column_ref[i * LANES : (i + 1) * LANES, :] = jnp.transpose(weight)
@@ -266,10 +294,10 @@
 
 
 def grid_last_kernel(
-    dims, code_s, count_s, column_ref, moved_ref, first_ref, field_ref, keep_ref, give_ref,
-    total, first_v, moved_v, pixf, field_v, gram_v, first_sems, block_sems, out_sem
+    dims, code_ref, count_ref, column_any, moved_ref, first_ref, field_ref, keep_ref, give_ref,
+    code_s, count_s, column_ref, total, first_v, moved_v, pixf, field_v, gram_v, small_sems, first_sems, block_sems, out_sem
 ):
-    time_count, space_count, rows_tm, slot_rows, first_rows, width = dims
+    time_count, space_count, rows_tm, slot_rows, first_rows, width, (meta_rows, folded) = dims
     blocks = time_count * space_count
     last_rows = slot_rows - first_rows
     group = rows_tm // STEPS
@@ -282,8 +310,12 @@
     def fetch(b):
         return pltpu.make_async_copy(moved_ref.at[b], moved_v.at[b], block_sems.at[b])
 
-    for b in range(blocks):
-        pl.when(count_s[b, 0] > first_rows)(fetch(b).start)
+    small = [
+        pltpu.make_async_copy(source, target, small_sems.at[i])
+        for i, (source, target) in enumerate(((count_ref, count_s), (code_ref, code_s), (column_any, column_ref)))
+    ]
+    for copy in small:
+        copy.start()
     for i in range(STEPS):
         load(i).start()
 
@@ -291,8 +323,14 @@
         total[pl.ds(pl.multiple_of(i * DAYS, DAYS), DAYS), :] = jnp.zeros((DAYS, LANES), jnp.float32)
         return 0
 
-    lax.fori_loop(0, rows_tm, clear, 0)
+    lax.fori_loop(0, rows_tm // 2, clear, 0)
+    small[0].wait()
+    for b in range(blocks):
+        pl.when(count_s[b, 0] > first_rows)(fetch(b).start)
+    lax.fori_loop(rows_tm // 2, rows_tm, clear, 0)
     total[rows_tm * DAYS :, :] = jnp.zeros((8, LANES), jnp.float32)
+    small[1].wait()
+    small[2].wait()
     for b in range(blocks):
 
         @pl.when(count_s[b, 0] > first_rows)
@@ -351,7 +389,7 @@
     last_rows = slot_rows - first_rows
     width = round_up(slots, LANES)
     blocks = time_count * space_count
-    dims = (time_count, space_count, rows_tm, slot_rows, first_rows, width)
+    dims = (time_count, space_count, rows_tm, slot_rows, first_rows, width, meta_layout(slots))
     codes = (blocks * width // LANES, LANES)
     rest = (codes[0] - first_rows // LANES * blocks, LANES)
     counts = (blocks, LANES)
@@ -360,7 +398,7 @@
     half = (DAYS // LANES // 2, RANK, LANES)
     params = pltpu.CompilerParams(vmem_limit_bytes=VMEM)
     moved_first, moved_last = (pltpu.with_memory_space_constraint(v, pltpu.VMEM) for v in (moved_first, moved_last))
-    total, _, code, count, column = pl.pallas_call(
+    total, _, rest_code, count, column = pl.pallas_call(
         functools.partial(grid_first_kernel, dims),
         out_shape=[
             jax.ShapeDtypeStruct(sums, jnp.float32),
@@ -370,7 +408,7 @@
             jax.ShapeDtypeStruct(columns, jnp.float32),
         ],
         scratch_shapes=[
-            pltpu.VMEM((blocks * META_ROWS, LANES), jnp.float32),
+            pltpu.VMEM((blocks * meta_layout(slots)[0], LANES), jnp.float32),
             pltpu.VMEM((blocks * first_rows, LANES), jnp.float32),
             pltpu.SMEM(codes, jnp.int32),
             pltpu.SMEM(counts, jnp.int32),
@@ -384,12 +422,9 @@
     return pl.pallas_call(
         functools.partial(grid_last_kernel, dims),
         in_specs=[
-            pl.BlockSpec(memory_space=pltpu.SMEM),
-            pl.BlockSpec(memory_space=pltpu.SMEM),
-            whole,
             pl.BlockSpec(memory_space=pl.ANY),
-            pl.BlockSpec(memory_space=pl.ANY),
-        ],
+        ]
+        * 5,
         out_specs=[pl.BlockSpec(memory_space=pl.ANY), whole, whole],
         out_shape=[
             jax.ShapeDtypeStruct((rows_tm, DAYS, LANES), jnp.bfloat16),
@@ -397,19 +432,23 @@
             pltpu.VMEM(half, jnp.float32),
         ],
         scratch_shapes=[
+            pltpu.SMEM(rest, jnp.int32),
+            pltpu.SMEM(counts, jnp.int32),
+            pltpu.VMEM(columns, jnp.float32),
             pltpu.VMEM(sums, jnp.float32),
             pltpu.VMEM((rows_tm * DAYS, LANES), jnp.float32),
             pltpu.VMEM((blocks, last_rows, LANES), jnp.bfloat16),
             pltpu.VMEM((blocks * last_rows, LANES), jnp.float32),
             pltpu.VMEM((rows_tm, DAYS, LANES), jnp.bfloat16),
             pltpu.VMEM((DAYS // LANES, RANK, LANES), jnp.float32),
+            pltpu.SemaphoreType.DMA((3,)),
             pltpu.SemaphoreType.DMA((STEPS,)),
             pltpu.SemaphoreType.DMA((blocks,)),
             pltpu.SemaphoreType.DMA,
         ],
         compiler_params=params,
         name="grid_last_and_gram",
-    )(code, count, column, moved_last, total)
+    )(rest_code, count, column, moved_last, total)
 
 
 def dot_f32(a, b, dims=(((1,), (0,)), ((), ()))):
@@ -423,13 +462,9 @@
     left, right = dims[0][0][0], dims[0][1][0]
     a_all = jnp.concatenate([a_high, a_high, a_low], axis=left)
     b_all = jnp.concatenate([b_high, b_low, b_high], axis=right)
-    return lax.dot_general(a_all, b_all, dims, preferred_element_type=jnp.float32)
-
-
-def invert(x):
-    guess = pl.reciprocal(x, approx=True)
-    guess = guess * (2.0 - x * guess)
-    return guess * (2.0 - x * guess)
+    half = a.shape[0] // 2
+    parts = [lax.dot_general(p, b_all, dims, preferred_element_type=jnp.float32) for p in (a_all[:half], a_all[half:])]
+    return jnp.concatenate(parts, axis=0)
 
 
 def lower_inverse(a):
@@ -451,7 +486,7 @@
         for s in range(0, 8, 2):
             p, q, r = e[s, s], e[s + 1, s], e[s + 1, s + 1]
             det = p * r - q * q
-            inv = invert(det)
+            inv = pl.reciprocal(det, approx=True)
             factors = {}
             for i in range(s + 2, 8):
                 x, y = e[i, s], e[i, s + 1]

time: 150 us -> 144 us (0.960)
  blocking collectives: 79.2 us -> 76 us
    pallas_call x1, Pallas kernels: 11.3 us -> 8.21 us  [pack(): pl.pallas_call(functools.partial(pack_kernel, (time_count, space_count, r...]
    pallas_call x1, Pallas kernels: 8.27 us -> 10.9 us  [grid_rows(): pl.pallas_call(functools.partial(grid_last_kernel, dims), in_specs=[pl.Bl...]
    all_to_all x1, blocking collectives: 14.9 us -> 13 us  [body(): mine = jnp.sum(among(pieces), axis=0, keepdims=True)]
    pallas_call x1, Pallas kernels: 19.5 us -> 17.8 us  [solve(): pl.pallas_call(functools.partial(solve_kernel, math.sqrt(cell_total)), in...]
  transfers between devices with their start and end apart: 3 -> 3, of which waited for: 3 -> 3; matrix products, arithmetic and copies ran while one was open for 0% -> 0% of each run, Pallas kernels for 12% -> 13%
where the time goes in v1:
time: 144 us
  blocking collectives  76 us (53%)
  Pallas kernels  56.3 us (39%)
  waiting for transfers between devices  8.47 us (6%)
  starting transfers between devices  2.71 us (2%)
    all_to_all x1, blocking collectives, body(): first = lax.all_to_all(first, axes, split_axis=0, concat_axis=0, tiled=True)  50.4 us
    pallas_call x1, Pallas kernels, grid_rows(): pl.pallas_call(functools.partial(grid_first_kernel, dims), out_shape=[jax...  19.4 us
    pallas_call x1, Pallas kernels, solve(): pl.pallas_call(functools.partial(solve_kernel, math.sqrt(cell_total)), in...  17.8 us
    all_to_all x1, blocking collectives, body(): mine = jnp.sum(among(pieces), axis=0, keepdims=True)  13 us
    all_to_all x1, blocking collectives, body(): own = among(jnp.broadcast_to(mine, pieces.shape)).reshape(keep.shape)  12.6 us
    pallas_call x1, Pallas kernels, grid_rows(): pl.pallas_call(functools.partial(grid_last_kernel, dims), in_specs=[pl.Bl...  10.9 us
    pallas_call x1, Pallas kernels, pack(): pl.pallas_call(functools.partial(pack_kernel, (time_count, space_count, r...  8.21 us
    all_to_all x1, waiting for transfers between devices, body(): last = lax.all_to_all(last, axes, split_axis=0, concat_axis=0, tiled=True)  5.42 us
  transfers between devices with their start and end apart: 3, of which 3 were waited for; matrix products, arithmetic and copies ran while one was open for 0% of the time, Pallas kernels for 13%

profile of v1, /device:TPU:0, one launch (start us, length us, event | category | flops | bytes accessed | tf_op | source)
XLA Modules:
  0.0 144.4 jit_solution(4880813517667678059)
XLA Ops:
  0.6 8.2 %pack.1 = (bf16[32,216,128]{2,1,0:T(8,128)(2,1)}, bf16[32,112,128]{2,1,0:T(8,128)(2,1)}) custom-call(s32[40,128]{1,0:T(8,128)} %bitcast.12, s32[40,128]{1,0:T(8,128)} %bitcast.13, s32[40,128]{1,0:T(8,128)} %bitcast.14, bf16[40,128]{1,0:T(8,128)(2,1)} %bitcast.15, bf16[5120,128]{1,0:T(8,128)(2,1)} %pix_ref.1), custom_call_target="tpu_custom_call" | custom-call | tf_op jit(solution)/shard_map/pack/pallas_call | solution.py:153
  8.8 50.4 %all_to_all.20.moved_ref = bf16[32,216,128]{2,1,0:T(8,128)(2,1)S(1)} all-to-all(bf16[32,216,128]{2,1,0:T(8,128)(2,1)} %get-tuple-element.14), channel_id=1, replica_groups=mesh['tm'=4,'space'=8] {'tm','space'}, dimensions={0} | all-to-all | bytes 3538944 | tf_op jit(solution)/shard_map/all_to_all | solution.py:621
  59.2 2.6 %all-to-all-start.1 = ((bf16[32,112,128]{2,1,0:T(8,128)(2,1)}), bf16[32,112,128]{2,1,0:T(8,128)(2,1)S(1)}, u32[]{:S(2)}, u32[]{:S(2)}) async-start(bf16[32,112,128]{2,1,0:T(8,128)(2,1)} %get-tuple-element.18), calls=%async_computation.1 | async-start | bytes 1835008 | tf_op jit(solution)/shard_map/all_to_all | solution.py:622
  61.8 19.4 %grid_first.1 = (f32[20488,128]{1,0:T(8,128)}, s32[96,128]{1,0:T(8,128)}, s32[64,128]{1,0:T(8,128)}, s32[32,128]{1,0:T(8,128)}, f32[384,32]{1,0:T(8,128)}) custom-call(bf16[32,216,128]{2,1,0:T(8,128)(2,1)S(1)} %all_to_all.20.moved_ref), custom_call_target="tpu_custom_call" | custom-call | bytes 60000000 | tf_op jit(solution)/shard_map/grid_first/pallas_call | solution.py:401
  81.2 5.4 %all-to-all-done.1.moved_ref = bf16[32,112,128]{2,1,0:T(8,128)(2,1)S(1)} async-done(((bf16[32,112,128]{2,1,0:T(8,128)(2,1)}), bf16[32,112,128]{2,1,0:T(8,128)(2,1)S(1)}, u32[]{:S(2)}, u32[]{:S(2)}) %all-to-all-start.1) | async-done | bytes 917536 | tf_op jit(solution)/shard_map/all_to_all | solution.py:622
  86.6 10.9 %grid_last_and_gram.1 = (bf16[40,512,128]{2,1,0:T(8,128)(2,1)}, f32[2,256,128]{2,1,0:T(8,128)S(1)}, f32[2,256,128]{2,1,0:T(8,128)S(1)}) custom-call(s32[64,128]{1,0:T(8,128)} %get-tuple-element.15.code_ref, s32[32,128]{1,0:T(8,128)} %get-tuple-element.16.count_ref, f32[384,32]{1,0:T(8,128)} %get-tuple-element.17.column_any, ...), custom_call_target="tpu_custom_call" | custom-call | tf_op jit(solution)/shard_map/grid_last_and_gram/pallas_call | solution.py:422
  97.6 0.1 collective-permute-start
  97.7 1.5 %collective-permute-done = f32[2,256,128]{2,1,0:T(8,128)S(1)} collective-permute-done((f32[2,256,128]{2,1,0:T(8,128)S(1)}, f32[2,256,128]{2,1,0:T(8,128)S(1)}, u32[]{:S(2)}, u32[]{:S(2)}) %collective-permute-start) | collective-permute-done | bytes 262176 | tf_op jit(solution)/shard_map/ppermute | solution.py:630
  99.2 13.0 %all_to_all.21 = f32[16,32,128]{2,1,0:T(8,128)S(1)} all-to-all(f32[16,32,128]{2,1,0:T(8,128)S(1)} %bitcast.11), channel_id=1, replica_groups={{0,1,2,3,4,5,6,7,16,17,18,19,20,21,22,23},{8,9,10,11,12,13,14,15,24,25,..., dimensions={0} | all-to-all | bytes 524288 | tf_op jit(solution)/shard_map/all_to_all | solution.py:631
  112.3 12.6 %all_to_all.22 = f32[16,32,128]{2,1,0:T(8,128)S(1)} all-to-all(f32[16,32,128]{2,1,0:T(8,128)S(1)} %broadcast_in_dim.13), channel_id=1, replica_groups={{0,1,2,3,4,5,6,7,16,17,18,19,20,21,22,23},{8,9,10,11,12,13,14,15,24,25,..., dimensions={0} | all-to-all | bytes 524288 | tf_op jit(solution)/shard_map/all_to_all | solution.py:632
  125.0 0.0 collective-permute-start.1
  125.0 1.5 %collective-permute-done.1.other_ref = f32[2,256,128]{2,1,0:T(8,128)S(1)} collective-permute-done((f32[2,256,128]{2,1,0:T(8,128)S(1)}, f32[2,256,128]{2,1,0:T(8,128)S(1)}, u32[]{:S(2)}, u32[]{:S(2)}) %collective-permute-start.1) | collective-permute-done | bytes 262176 | tf_op jit(solution)/shard_map/ppermute | solution.py:633
  126.5 17.8 %factor_basis_and_polar.1 = (bf16[40,256,128]{2,1,0:T(8,128)(2,1)}, f32[256,256]{1,0:T(8,128)}) custom-call(f32[2,256,128]{2,1,0:T(8,128)S(1)} %bitcast.9, f32[2,256,128]{2,1,0:T(8,128)S(1)} %collective-permute-done.1.other_ref, bf16[40,512,128]{2,1,0:T(8,128)(2,1)} %get-tuple-element.20.field_ref), custom_call_target="tpu_custom_call" | custom-call | tf_op jit(solution)/shard_map/factor_basis_and_polar/pallas_call | solution.py:592
  (3 shorter events, 0.1 us)
Async XLA Ops:
  59.2 27.4 %all-to-all-start.1 = ((bf16[32,112,128]{2,1,0:T(8,128)(2,1)}), bf16[32,112,128]{2,1,0:T(8,128)(2,1)S(1)}, u32[]{:S(2)}, u32[]{:S(2)}) async-start(bf16[32,112,128]{2,1,0:T(8,128)(2,1)} %get-tuple-element.18), calls=%async_computation.1 | async-start | bytes 1835008 | tf_op jit(solution)/shard_map/all_to_all | solution.py:622
  97.6 1.6 %collective-permute-start = (f32[2,256,128]{2,1,0:T(8,128)S(1)}, f32[2,256,128]{2,1,0:T(8,128)S(1)}, u32[]{:S(2)}, u32[]{:S(2)}) collective-permute-start(f32[2,256,128]{2,1,0:T(8,128)S(1)} %get-tuple-element.22), channel_id=1, source_target_pairs={{0,8},{8,0},{16,24},{24,16},{1,9},{9,1},{17,25},{25,17},{2,10},{10... | collective-permute-start | bytes 786440 | tf_op jit(solution)/shard_map/ppermute | solution.py:630
  125.0 1.5 %collective-permute-start.1 = (f32[2,256,128]{2,1,0:T(8,128)S(1)}, f32[2,256,128]{2,1,0:T(8,128)S(1)}, u32[]{:S(2)}, u32[]{:S(2)}) collective-permute-start(f32[2,256,128]{2,1,0:T(8,128)S(1)} %bitcast.8), channel_id=1, source_target_pairs={{0,8},{8,0},{16,24},{24,16},{1,9},{9,1},{17,25},{25,17},{2,10},{10... | collective-permute-start | bytes 786440 | tf_op jit(solution)/shard_map/ppermute | solution.py:633

commit v2 on v1

--- a/solution.py
+++ b/solution.py
@@ -99,7 +99,7 @@
         hot = dest_number == dest
         place = jnp.where(slot_number == rank, 1.0, 0.0).astype(jnp.bfloat16)
         values = jnp.concatenate([jnp.where(hot, v, 0.0) for v in (weight, local_row, day)], axis=0).astype(jnp.bfloat16)
-        meta_v[...] += lax.dot_general(values, place, LAST_LAST, preferred_element_type=jnp.float32)
+        meta_v[...] += lax.dot_general(place, values, LAST_LAST, preferred_element_type=jnp.float32)
         for half in range(2):
             for lane in range(LANES):
                 outf[pl.ds(pos_s[2 * c + half, lane], 1), :] = pixf[pl.ds(base + half * LANES + lane, 1), :]
@@ -108,8 +108,10 @@
     lax.fori_loop(0, chunks // 2, move, 0)
     whole = pieces - 1 if folded else pieces
 
+    turned = [jnp.transpose(meta_v[i * LANES : (i + 1) * LANES, :]) for i in range(pieces)]
+
     def lanes(v, i):
-        return meta_v[v * dest_count : (v + 1) * dest_count, i * LANES : (i + 1) * LANES]
+        return turned[i][v * dest_count : (v + 1) * dest_count, :]
 
     def put(at, value):
         mrow[pl.ds(at, dest_count, stride=meta_rows), :] = value
@@ -159,7 +161,7 @@
             pltpu.VMEM(shape, jnp.int32),
             pltpu.SMEM(shape, jnp.int32),
             pltpu.VMEM((5,) + shape, jnp.float32),
-            pltpu.VMEM((3 * dest_count, width), jnp.float32),
+            pltpu.VMEM((width, 3 * dest_count), jnp.float32),
             pltpu.VMEM((swath_rows, LANES), jnp.float32),
             pltpu.VMEM((dest_count * slot_rows, LANES), jnp.float32),
             pltpu.VMEM((dest_count * layout[0], LANES), jnp.float32),
@@ -294,8 +296,8 @@
 
 
 def grid_last_kernel(
-    dims, code_ref, count_ref, column_any, moved_ref, first_ref, field_ref, keep_ref, give_ref,
-    code_s, count_s, column_ref, total, first_v, moved_v, pixf, field_v, gram_v, small_sems, first_sems, block_sems, out_sem
+    dims, code_s, count_s, column_ref, moved_ref, first_ref, field_ref, keep_ref, give_ref,
+    total, first_v, moved_v, pixf, field_v, gram_v, first_sems, block_sems, out_sem
 ):
     time_count, space_count, rows_tm, slot_rows, first_rows, width, (meta_rows, folded) = dims
     blocks = time_count * space_count
@@ -310,12 +312,8 @@
     def fetch(b):
         return pltpu.make_async_copy(moved_ref.at[b], moved_v.at[b], block_sems.at[b])
 
-    small = [
-        pltpu.make_async_copy(source, target, small_sems.at[i])
-        for i, (source, target) in enumerate(((count_ref, count_s), (code_ref, code_s), (column_any, column_ref)))
-    ]
-    for copy in small:
-        copy.start()
+    for b in range(blocks):
+        pl.when(count_s[b, 0] > first_rows)(fetch(b).start)
     for i in range(STEPS):
         load(i).start()
 
@@ -323,14 +321,8 @@
         total[pl.ds(pl.multiple_of(i * DAYS, DAYS), DAYS), :] = jnp.zeros((DAYS, LANES), jnp.float32)
         return 0
 
-    lax.fori_loop(0, rows_tm // 2, clear, 0)
-    small[0].wait()
-    for b in range(blocks):
-        pl.when(count_s[b, 0] > first_rows)(fetch(b).start)
-    lax.fori_loop(rows_tm // 2, rows_tm, clear, 0)
+    lax.fori_loop(0, rows_tm, clear, 0)
     total[rows_tm * DAYS :, :] = jnp.zeros((8, LANES), jnp.float32)
-    small[1].wait()
-    small[2].wait()
     for b in range(blocks):
 
         @pl.when(count_s[b, 0] > first_rows)
@@ -422,9 +414,12 @@
     return pl.pallas_call(
         functools.partial(grid_last_kernel, dims),
         in_specs=[
+            pl.BlockSpec(memory_space=pltpu.SMEM),
+            pl.BlockSpec(memory_space=pltpu.SMEM),
+            whole,
             pl.BlockSpec(memory_space=pl.ANY),
-        ]
-        * 5,
+            pl.BlockSpec(memory_space=pl.ANY),
+        ],
         out_specs=[pl.BlockSpec(memory_space=pl.ANY), whole, whole],
         out_shape=[
             jax.ShapeDtypeStruct((rows_tm, DAYS, LANES), jnp.bfloat16),
@@ -432,16 +427,12 @@
             pltpu.VMEM(half, jnp.float32),
         ],
         scratch_shapes=[
-            pltpu.SMEM(rest, jnp.int32),
-            pltpu.SMEM(counts, jnp.int32),
-            pltpu.VMEM(columns, jnp.float32),
             pltpu.VMEM(sums, jnp.float32),
             pltpu.VMEM((rows_tm * DAYS, LANES), jnp.float32),
             pltpu.VMEM((blocks, last_rows, LANES), jnp.bfloat16),
             pltpu.VMEM((blocks * last_rows, LANES), jnp.float32),
             pltpu.VMEM((rows_tm, DAYS, LANES), jnp.bfloat16),
             pltpu.VMEM((DAYS // LANES, RANK, LANES), jnp.float32),
-            pltpu.SemaphoreType.DMA((3,)),
             pltpu.SemaphoreType.DMA((STEPS,)),
             pltpu.SemaphoreType.DMA((blocks,)),
             pltpu.SemaphoreType.DMA,
@@ -451,20 +442,33 @@
     )(rest_code, count, column, moved_last, total)
 
 
+def bf16_parts(x, count):
+    found = []
+    for _ in range(count):
+        found.append(x.astype(jnp.bfloat16))
+        x = x - found[-1].astype(jnp.float32)
+    return found
+
+
+def dot_parts(a, b, dims, count, splits):
+    (left,), (right,) = dims[0]
+    a_parts, b_parts = bf16_parts(a, count), bf16_parts(b, count)
+    pairs = [(i, j) for i in range(count) for j in range(count - i)]
+    a_all = jnp.concatenate([a_parts[i] for i, _ in pairs], axis=left)
+    b_all = jnp.concatenate([b_parts[j] for _, j in pairs], axis=right)
+    dot = functools.partial(lax.dot_general, dimension_numbers=dims, preferred_element_type=jnp.float32)
+    if splits == 1:
+        return dot(a_all, b_all)
+    size = a.shape[0] // splits
+    return jnp.concatenate([dot(a_all[i * size : (i + 1) * size], b_all) for i in range(splits)], axis=0)
+
+
 def dot_f32(a, b, dims=(((1,), (0,)), ((), ()))):
-    return lax.dot_general(a, b, dims, precision=lax.Precision.HIGHEST, preferred_element_type=jnp.float32)
+    return dot_parts(a, b, dims, 3, 1)
 
 
 def dot_three(a, b, dims=(((1,), (0,)), ((), ()))):
-    a_high, b_high = a.astype(jnp.bfloat16), b.astype(jnp.bfloat16)
-    a_low = (a - a_high.astype(jnp.float32)).astype(jnp.bfloat16)
-    b_low = (b - b_high.astype(jnp.float32)).astype(jnp.bfloat16)
-    left, right = dims[0][0][0], dims[0][1][0]
-    a_all = jnp.concatenate([a_high, a_high, a_low], axis=left)
-    b_all = jnp.concatenate([b_high, b_low, b_high], axis=right)
-    half = a.shape[0] // 2
-    parts = [lax.dot_general(p, b_all, dims, preferred_element_type=jnp.float32) for p in (a_all[:half], a_all[half:])]
-    return jnp.concatenate(parts, axis=0)
+    return dot_parts(a, b, dims, 2, 4)
 
 
 def lower_inverse(a):

time: 144 us -> 146 us (1.014)
    pallas_call x1, Pallas kernels: 17.8 us -> 19.9 us  [solve(): pl.pallas_call(functools.partial(solve_kernel, math.sqrt(cell_total)), in...]
    pallas_call x1, Pallas kernels: 10.9 us -> 9.2 us  [grid_rows(): pl.pallas_call(functools.partial(grid_last_kernel, dims), in_specs=[pl.Bl...]
where the time goes in v2:
time: 146 us; the launch traced here: 145 us
  blocking collectives  76 us (52%)
  Pallas kernels  56.4 us (39%)
  waiting for transfers between devices  9.01 us (6%)
  starting transfers between devices  2.71 us (2%)
    all_to_all x1, blocking collectives, body(): first = lax.all_to_all(first, axes, split_axis=0, concat_axis=0, tiled=True)  50.4 us
    pallas_call x1, Pallas kernels, solve(): pl.pallas_call(functools.partial(solve_kernel, math.sqrt(cell_total)), in...  19.9 us
    pallas_call x1, Pallas kernels, grid_rows(): pl.pallas_call(functools.partial(grid_first_kernel, dims), out_shape=[jax...  18.8 us
    all_to_all x1, blocking collectives, body(): mine = jnp.sum(among(pieces), axis=0, keepdims=True)  13 us
    all_to_all x1, blocking collectives, body(): own = among(jnp.broadcast_to(mine, pieces.shape)).reshape(keep.shape)  12.6 us
    pallas_call x1, Pallas kernels, grid_rows(): pl.pallas_call(functools.partial(grid_last_kernel, dims), in_specs=[pl.Bl...  9.2 us
    pallas_call x1, Pallas kernels, pack(): pl.pallas_call(functools.partial(pack_kernel, (time_count, space_count, r...  8.48 us
    all_to_all x1, waiting for transfers between devices, body(): last = lax.all_to_all(last, axes, split_axis=0, concat_axis=0, tiled=True)  5.95 us
  transfers between devices with their start and end apart: 3, of which 3 were waited for; matrix products, arithmetic and copies ran while one was open for 0% of the time, Pallas kernels for 13%

profile of v2, /device:TPU:0, one launch (start us, length us, event | category | flops | bytes accessed | tf_op | source)
XLA Modules:
  0.0 145.1 jit_solution(1365408105180268133)
XLA Ops:
  0.6 8.5 %pack.1 = (bf16[32,216,128]{2,1,0:T(8,128)(2,1)}, bf16[32,112,128]{2,1,0:T(8,128)(2,1)}) custom-call(s32[40,128]{1,0:T(8,128)} %bitcast.12, s32[40,128]{1,0:T(8,128)} %bitcast.13, s32[40,128]{1,0:T(8,128)} %bitcast.14, bf16[40,128]{1,0:T(8,128)(2,1)} %bitcast.15, bf16[5120,128]{1,0:T(8,128)(2,1)} %pix_ref.1), custom_call_target="tpu_custom_call" | custom-call | tf_op jit(solution)/shard_map/pack/pallas_call | solution.py:155
  9.1 50.4 %all_to_all.20.moved_ref = bf16[32,216,128]{2,1,0:T(8,128)(2,1)S(1)} all-to-all(bf16[32,216,128]{2,1,0:T(8,128)(2,1)} %get-tuple-element.14), channel_id=1, replica_groups=mesh['tm'=4,'space'=8] {'tm','space'}, dimensions={0} | all-to-all | bytes 3538944 | tf_op jit(solution)/shard_map/all_to_all | solution.py:625
  59.5 2.6 %all-to-all-start.1 = ((bf16[32,112,128]{2,1,0:T(8,128)(2,1)}), bf16[32,112,128]{2,1,0:T(8,128)(2,1)S(1)}, u32[]{:S(2)}, u32[]{:S(2)}) async-start(bf16[32,112,128]{2,1,0:T(8,128)(2,1)} %get-tuple-element.18), calls=%async_computation.1 | async-start | bytes 1835008 | tf_op jit(solution)/shard_map/all_to_all | solution.py:626
  62.1 18.8 %grid_first.1 = (f32[20488,128]{1,0:T(8,128)}, s32[96,128]{1,0:T(8,128)}, s32[64,128]{1,0:T(8,128)}, s32[32,128]{1,0:T(8,128)}, f32[384,32]{1,0:T(8,128)}) custom-call(bf16[32,216,128]{2,1,0:T(8,128)(2,1)S(1)} %all_to_all.20.moved_ref), custom_call_target="tpu_custom_call" | custom-call | bytes 60000000 | tf_op jit(solution)/shard_map/grid_first/pallas_call | solution.py:393
  80.9 6.0 %all-to-all-done.1.moved_ref = bf16[32,112,128]{2,1,0:T(8,128)(2,1)S(1)} async-done(((bf16[32,112,128]{2,1,0:T(8,128)(2,1)}), bf16[32,112,128]{2,1,0:T(8,128)(2,1)S(1)}, u32[]{:S(2)}, u32[]{:S(2)}) %all-to-all-start.1) | async-done | bytes 917536 | tf_op jit(solution)/shard_map/all_to_all | solution.py:626
  86.9 9.2 %grid_last_and_gram.1 = (bf16[40,512,128]{2,1,0:T(8,128)(2,1)}, f32[2,256,128]{2,1,0:T(8,128)S(1)}, f32[2,256,128]{2,1,0:T(8,128)S(1)}) custom-call(s32[64,128]{1,0:T(8,128)} %get-tuple-element.15.code_s, s32[32,128]{1,0:T(8,128)} %get-tuple-element.16.count_s, f32[384,32]{1,0:T(8,128)} %get-tuple-element.17.column_ref, ...), custom_call_target="tpu_custom_call" | custom-call | tf_op jit(solution)/shard_map/grid_last_and_gram/pallas_call | solution.py:414
  96.1 0.1 collective-permute-start
  96.2 1.5 %collective-permute-done = f32[2,256,128]{2,1,0:T(8,128)S(1)} collective-permute-done((f32[2,256,128]{2,1,0:T(8,128)S(1)}, f32[2,256,128]{2,1,0:T(8,128)S(1)}, u32[]{:S(2)}, u32[]{:S(2)}) %collective-permute-start) | collective-permute-done | bytes 262176 | tf_op jit(solution)/shard_map/ppermute | solution.py:634
  97.7 13.0 %all_to_all.21 = f32[16,32,128]{2,1,0:T(8,128)S(1)} all-to-all(f32[16,32,128]{2,1,0:T(8,128)S(1)} %bitcast.11), channel_id=1, replica_groups={{0,1,2,3,4,5,6,7,16,17,18,19,20,21,22,23},{8,9,10,11,12,13,14,15,24,25,..., dimensions={0} | all-to-all | bytes 524288 | tf_op jit(solution)/shard_map/all_to_all | solution.py:635
  110.8 12.6 %all_to_all.22 = f32[16,32,128]{2,1,0:T(8,128)S(1)} all-to-all(f32[16,32,128]{2,1,0:T(8,128)S(1)} %broadcast_in_dim.13), channel_id=1, replica_groups={{0,1,2,3,4,5,6,7,16,17,18,19,20,21,22,23},{8,9,10,11,12,13,14,15,24,25,..., dimensions={0} | all-to-all | bytes 524288 | tf_op jit(solution)/shard_map/all_to_all | solution.py:636
  123.5 0.0 collective-permute-start.1
  123.5 1.5 %collective-permute-done.1.other_ref = f32[2,256,128]{2,1,0:T(8,128)S(1)} collective-permute-done((f32[2,256,128]{2,1,0:T(8,128)S(1)}, f32[2,256,128]{2,1,0:T(8,128)S(1)}, u32[]{:S(2)}, u32[]{:S(2)}) %collective-permute-start.1) | collective-permute-done | bytes 262176 | tf_op jit(solution)/shard_map/ppermute | solution.py:637
  125.0 19.9 %factor_basis_and_polar.1 = (bf16[40,256,128]{2,1,0:T(8,128)(2,1)}, f32[256,256]{1,0:T(8,128)}) custom-call(f32[2,256,128]{2,1,0:T(8,128)S(1)} %bitcast.9, f32[2,256,128]{2,1,0:T(8,128)S(1)} %collective-permute-done.1.other_ref, bf16[40,512,128]{2,1,0:T(8,128)(2,1)} %get-tuple-element.20.field_ref), custom_call_target="tpu_custom_call" | custom-call | tf_op jit(solution)/shard_map/factor_basis_and_polar/pallas_call | solution.py:596
  (3 shorter events, 0.1 us)
Async XLA Ops:
  59.5 27.4 %all-to-all-start.1 = ((bf16[32,112,128]{2,1,0:T(8,128)(2,1)}), bf16[32,112,128]{2,1,0:T(8,128)(2,1)S(1)}, u32[]{:S(2)}, u32[]{:S(2)}) async-start(bf16[32,112,128]{2,1,0:T(8,128)(2,1)} %get-tuple-element.18), calls=%async_computation.1 | async-start | bytes 1835008 | tf_op jit(solution)/shard_map/all_to_all | solution.py:626
  96.1 1.6 %collective-permute-start = (f32[2,256,128]{2,1,0:T(8,128)S(1)}, f32[2,256,128]{2,1,0:T(8,128)S(1)}, u32[]{:S(2)}, u32[]{:S(2)}) collective-permute-start(f32[2,256,128]{2,1,0:T(8,128)S(1)} %get-tuple-element.22), channel_id=1, source_target_pairs={{0,8},{8,0},{16,24},{24,16},{1,9},{9,1},{17,25},{25,17},{2,10},{10... | collective-permute-start | bytes 786440 | tf_op jit(solution)/shard_map/ppermute | solution.py:634
  123.5 1.5 %collective-permute-start.1 = (f32[2,256,128]{2,1,0:T(8,128)S(1)}, f32[2,256,128]{2,1,0:T(8,128)S(1)}, u32[]{:S(2)}, u32[]{:S(2)}) collective-permute-start(f32[2,256,128]{2,1,0:T(8,128)S(1)} %bitcast.8), channel_id=1, source_target_pairs={{0,8},{8,0},{16,24},{24,16},{1,9},{9,1},{17,25},{25,17},{2,10},{10... | collective-permute-start | bytes 786440 | tf_op jit(solution)/shard_map/ppermute | solution.py:637
